TPU v7x, 128 devices: a whole 4x4x4 slice. The times are simulated.
128 devices in a mesh: grp: 4 (over y), dev: 32 (over z, x, core).
Axes of the slice: x: 4, y: 4, z: 4, core: 2. Of those that a mesh axis runs over, the one named last changes fastest.
Arguments:
- points: float32 [64, 196608], P(None, 'dev'), may hold values from -6 to 6
- weights: float32 [196608, 128], P('dev'), may hold values from -4 to 4
- proj: float32 [256, 196608], P(None, 'dev'), may hold values from -0.078125 to 0.078125
- fetch_table: int32 [3, 32, 32, 2], P(None, 'dev'), may hold values from 0 to 11, as said below
- near_list: int32 [384, 16], P('dev'), may hold values from 0 to 63, as said below
- far_list: int32 [384, 8], P('dev'), may hold values from 0 to 31, as said below
- skel_idx: int32 [32, 256], P('dev'), may hold values from 0 to 6143, as said below
Outputs:
- potential: float32 [196608, 128], P('dev')
Inputs may be any that keep to these rules, and one draw needn't show every extreme that they name: Entries of fetch_table[r, d, e] are distinct local leaf numbers of column e. `near_list`: the 16 slots of one target leaf are distinct. `far_list`: the 8 nodes of one target leaf are distinct, and one of them is node (c + 1) mod 32 for the leaf's column c. `skel_idx`: the 256 skeleton points of one node are distinct.
All inputs are finite; a program needn't handle non-finite values.
Results may differ from a plain program's by a relative error of at most 0.0003.
Values sent between devices are 32-bit elements; how exact they have to be, the bound alone decides.
A program may use at most 192 MiB of HBM per device.

v0:
```python
import jax
import jax.numpy as jnp
from jax import lax
from jax.sharding import PartitionSpec as P


def kernel_sum(target, sources, values):
    high = lax.Precision.HIGHEST
    inner = jnp.einsum("dt,jds->tjs", target, sources, precision=high)
    target_norm = jnp.sum(target * target, axis=0)
    source_norm = jnp.sum(sources * sources, axis=1)
    distance = target_norm[:, None, None] + source_norm[None] - 2.0 * inner
    kernel = jnp.exp(-distance * (2.0 / target.shape[0]))
    return jnp.einsum("tjs,jsw->tw", kernel, values, precision=high)


def on_device(points, weights, proj, fetch_table, near_list, far_list, skel_idx):
    features, column_points = points.shape
    columns = weights.shape[1]
    devices = lax.axis_size("dev")
    groups = lax.axis_size("grp")
    targets = near_list.shape[0]
    leaf_size = column_points // targets
    row_leaves = targets // (groups - 1)
    capacity = fetch_table.shape[3]
    skeleton = skel_idx.shape[1]
    group_index = lax.axis_index("grp")
    near_row = jnp.minimum(group_index, groups - 2)
    far_side = group_index == groups - 1
    leaf_coords = points.reshape(features, targets, leaf_size)
    leaf_weights = weights.reshape(targets, leaf_size, columns)
    requests = lax.dynamic_index_in_dim(fetch_table[:, 0], near_row, 0, keepdims=False)
    asked = lax.all_to_all(requests, "dev", split_axis=0, concat_axis=0, tiled=True)
    coords = jnp.moveaxis(jnp.take(leaf_coords, asked, axis=1), 0, 2)
    values = jnp.take(leaf_weights, asked, axis=0)
    fetched_coords = lax.all_to_all(coords, "dev", split_axis=0, concat_axis=0, tiled=True)
    fetched_values = lax.all_to_all(values, "dev", split_axis=0, concat_axis=0, tiled=True)
    flat_coords = fetched_coords.reshape(devices * capacity, features, leaf_size)
    flat_values = fetched_values.reshape(devices * capacity, leaf_size, columns)
    local_skeleton = jnp.take(points, skel_idx[0], axis=1)
    share_len = column_points // groups
    share_start = group_index * share_len
    share_proj = lax.dynamic_slice_in_dim(proj, share_start, share_len, 1)
    share_weights = lax.dynamic_slice_in_dim(weights, share_start, share_len, 0)
    partial_value = jnp.dot(
        share_proj,
        share_weights,
        preferred_element_type=jnp.float32,
        precision=lax.Precision.HIGHEST,
    )
    node_index = lax.axis_index("dev")
    owner_mask = jnp.where(far_side, 1.0, 0.0).astype(jnp.float32)
    table_coords = jnp.zeros((devices, features, skeleton), jnp.float32)
    table_coords = lax.dynamic_update_index_in_dim(
        table_coords, local_skeleton * owner_mask, node_index, 0
    )
    table_weights = jnp.zeros((devices, skeleton, columns), jnp.float32)
    table_weights = lax.dynamic_update_index_in_dim(table_weights, partial_value, node_index, 0)
    skel_coords, skel_weights = lax.psum((table_coords, table_weights), ("grp", "dev"))

    def near_work():
        slots = lax.dynamic_slice_in_dim(near_list, near_row * row_leaves, row_leaves, 0)
        leaf_numbers = near_row * row_leaves + jnp.arange(row_leaves, dtype=jnp.int32)

        def near_leaf(items):
            leaf_number, leaf_slots = items
            target = jnp.take(leaf_coords, leaf_number, axis=1)
            return kernel_sum(
                target,
                jnp.take(flat_coords, leaf_slots, axis=0),
                jnp.take(flat_values, leaf_slots, axis=0),
            )

        block = lax.map(near_leaf, (leaf_numbers, slots))
        empty = jnp.zeros((targets, leaf_size, columns), jnp.float32)
        return lax.dynamic_update_slice_in_dim(empty, block, near_row * row_leaves, 0)

    def far_work():

        def far_leaf(items):
            leaf_number, node_ids = items
            target = jnp.take(leaf_coords, leaf_number, axis=1)
            return kernel_sum(
                target,
                jnp.take(skel_coords, node_ids, axis=0),
                jnp.take(skel_weights, node_ids, axis=0),
            )

        return lax.map(far_leaf, (jnp.arange(targets, dtype=jnp.int32), far_list))

    contribution = lax.cond(far_side, far_work, near_work)
    total = lax.psum(contribution, "grp")
    return total.reshape(column_points, columns)


def solution(mesh):
    placed = (
        P(None, "dev"),
        P("dev", None),
        P(None, "dev"),
        P(None, "dev", None, None),
        P("dev", None),
        P("dev", None),
        P("dev", None),
    )
    return jax.shard_map(
        on_device, mesh=mesh, in_specs=placed, out_specs=P("dev", None), check_vma=False
    )
```

profile of v0, /device:TPU:1, one launch (start us, length us, event | category | flops | bytes accessed | tf_op | source)
XLA Modules:
  0.0 820.4 jit_solution(13350892789192930071)
XLA Ops:
  6.5 0.8 fusion.82
  7.4 0.7 copy.36
  8.1 9.4 %all-to-all-start = ((s32[32,1,2]{2,1,0:T(1,128)}), s32[32,1,2]{2,1,0:T(1,128)S(1)}, u32[]{:S(2)}, u32[]{:S(2)}) async-start(s32[32,1,2]{2,1,0:T(1,128)} %copy.36), calls=%async_computation | async-start | bytes 32768 | tf_op jit(solution)/shard_map/all_to_all | solution.py:33
  17.5 2.7 copy.64
  20.2 4.2 all-to-all-done
  24.4 0.1 copy.37
  24.5 0.1 copy.40
  24.6 0.1 reshape.285
  24.7 0.1 copy.38
  24.8 5.7 gather_fusion.4
  30.6 8.5 %broadcast_select_fusion.1 = f32[32,2,64,512]{3,2,1,0:T(8,128)} fusion(f32[32,2,64,512]{3,2,1,0:T(8,128)} %bitcast.103, pred[32,2]{1,0:T(8,128)(4,1)S(1)} %copy.38), kind=kLoop, calls=%fused_computation.87 | loop fusion | flops 2097152 | bytes 16777280 | tf_op jit(solution)/shard_map/jit(_take)/select_n | solution.py:34
  39.1 5.2 all-to-all-start.1
  44.3 7.4 gather_fusion.5
  51.6 11.6 %broadcast_select_fusion = f32[32,2,512,128]{3,2,1,0:T(8,128)} fusion(f32[32,2,512,128]{3,2,1,0:T(8,128)} %bitcast.101, pred[32,2]{1,0:T(8,128)(4,1)S(1)} %copy.38), kind=kLoop, calls=%fused_computation.86 | loop fusion | flops 4194304 | bytes 33554496 | tf_op jit(solution)/shard_map/jit(_take)/select_n | solution.py:35
  63.2 80.8 %all-to-all-done.1 = f32[32,2,64,512]{3,2,1,0:T(8,128)} async-done(((f32[32,2,64,512]{3,2,1,0:T(8,128)}), f32[32,2,64,512]{3,2,1,0:T(8,128)}, u32[]{:S(2)}, u32[]{:S(2)}) %all-to-all-start.1) | async-done | bytes 8388640 | tf_op jit(solution)/shard_map/all_to_all | solution.py:36
  144.0 11.3 %all-to-all-start.2 = ((f32[32,2,512,128]{3,2,1,0:T(8,128)}), f32[32,2,512,128]{3,2,1,0:T(8,128)}, u32[]{:S(2)}, u32[]{:S(2)}) async-start(f32[32,2,512,128]{3,2,1,0:T(8,128)} %broadcast_select_fusion), calls=%async_computation.2 | async-start | bytes 33554432 | tf_op jit(solution)/shard_map/all_to_all | solution.py:37
  155.3 0.0 all-reduce.6.cloned.1.call-start
  155.4 3.3 copy.43
  158.6 2.6 gather_fusion.6
  161.3 0.1 copy.44
  161.3 2.4 broadcast_in_dim.110
  163.8 3.5 fusion.75
  167.2 1.6 broadcast_in_dim.107
  168.8 0.6 fusion.80
  169.4 0.0 all-reduce.6.cloned.1.call-update
  169.5 0.0 all-reduce.4.cloned.1.call-start
  169.5 1.9 reshape.193
  171.4 310.3 %all-reduce.6.cloned.1.call-done = (f32[32,64,256]{2,1,0:T(8,128)}, f32[32,256,128]{2,1,0:T(8,128)}) async-done(((f32[32,64,256]{2,1,0:T(8,128)}, f32[32,256,128]{2,1,0:T(8,128)}), (f32[32,64,256]{2,1,0:T(8,128)}, f32[32,256,128]{2,1,0:T(8,128)})) %all-reduce.6.cloned.1.call-update) | async-done | bytes 6291472 | tf_op jit(solution)/shard_map/psum | solution.py:59
  481.8 223.2 %conditional.1 = (f32[12,512,128]{2,1,0:T(8,128)}) conditional(s32[]{:T(128)} %convert_element_type.3, (s32[]{:T(128)}, s32[12,16]{1,0:T(8,128)}, f32[32,2,64,512]{3,2,1,0:T(8,128)}, f32[32,2,512,128]{3,2,1,0:T(8,128)}, f32[64,12,512]{2,1,0:T(8,128)}) %tuple.20, (f32[64,12,512]{2,1,0:T(8,128)}, s32[12,8]{0,1:T(8,128)S(1)}, f32[32,64,256]{2,1,0:T(8,128)}, ...), branch_computations={%region_2.0_spmd, %region_7.13_spmd} | conditional | flops 9687917568 | bytes 60630836 | solution.py:91
  481.8 0.7 constant_dynamic-slice_fusion.2
  482.4 218.3 %while.19 = (s32[]{:T(128)}, f32[4,512,128]{2,1,0:T(8,128)}, s32[4]{0:T(128)S(1)}, f32[64,12,512]{2,1,0:T(8,128)}, s32[4,16]{1,0:T(4,128)S(1)}, /*index=5*/f32[6...) while((s32[]{:T(128)}, f32[4,512,128]{2,1,0:T(8,128)}, ...), condition=%wide.region_6.7_spmd, body=%wide.region_3.6_spmd.sunk | while | flops 9687917568 | bytes 55387260 | solution.py:74
  482.5 0.6 dynamic_slice.65
  484.9 1.3 constant_dynamic-slice_fusion.9
  486.3 4.1 gather_fusion.3
  490.4 16.2 %fusion.112 = f32[512,16,512]{2,0,1:T(8,128)} fusion(f32[16,64,512]{2,1,0:T(8,128)S(1)} %gather_fusion.3, pred[16]{0:T(512)(128)(4,1)S(1)} %compare_and_fusion.7, f32[64,1,512]{2,1,0:T(1,128)S(1)} %constant_dynamic-slice_fusion.9, pred[]{:T(512)S(6)} %and.57), kind=kOutput, calls=%fused_computation.22.clone.1 | convolution fusion | flops 3221782528 | bytes 19005456 | tf_op jit(solution)/shard_map/cond/branch_0_fun/while/body/eval_jaxpr/dt,jds->tjs/dot_general | solution.py:9
  506.6 0.4 multiply_reduce_fusion.5
  507.0 8.5 %gather_fusion.2 = f32[16,512,128]{2,1,0:T(8,128)} fusion(f32[64,512,128]{2,1,0:T(8,128)} %get-tuple-element.330, s32[1024]{0:T(1024)S(1)} %pad_clamp_fusion.7), kind=kCustom, calls=%fused_computation.1.clone.1 | custom fusion | bytes 8388672 | tf_op jit(solution)/shard_map/cond/branch_0_fun/while/body/eval_jaxpr/jit(_take)/gather | solution.py:71
  515.5 21.5 %fusion.114 = f32[4,512,128]{2,1,0:T(8,128)} fusion(f32[4,512,128]{2,1,0:T(8,128)} %get-tuple-element.314, s32[]{:T(128)} %get-tuple-element.313, f32[16,512,128]{2,1,0:T(8,128)} %gather_fusion.2, pred[16]{0:T(512)(128)(4,1)S(1)} %compare_and_fusion.7, f32[512,16,512]{2,0,1:T(8,128)} %fusion.112, f32[16,512]{1,0:T(8,128)S(1)} %multiply_reduce_fusion.5, ...), kind=kOutput, calls=%fused_computation.25.clone.1 | convolution fusion | flops 6464471040 | bytes 21269008 | tf_op jit(solution)/shard_map/cond/branch_0_fun/while/body/eval_jaxpr/tjs,jsw->tw/dot_general | solution.py:14
  537.0 0.6 dynamic_slice.65
  539.5 1.3 constant_dynamic-slice_fusion.9
  540.9 4.1 gather_fusion.3
  545.0 16.2 %fusion.112 = f32[512,16,512]{2,0,1:T(8,128)} fusion(f32[16,64,512]{2,1,0:T(8,128)S(1)} %gather_fusion.3, pred[16]{0:T(512)(128)(4,1)S(1)} %compare_and_fusion.7, f32[64,1,512]{2,1,0:T(1,128)S(1)} %constant_dynamic-slice_fusion.9, pred[]{:T(512)S(6)} %and.57), kind=kOutput, calls=%fused_computation.22.clone.1 | convolution fusion | flops 3221782528 | bytes 19005456 | tf_op jit(solution)/shard_map/cond/branch_0_fun/while/body/eval_jaxpr/dt,jds->tjs/dot_general | solution.py:9
  561.2 0.4 multiply_reduce_fusion.5
  561.5 8.5 %gather_fusion.2 = f32[16,512,128]{2,1,0:T(8,128)} fusion(f32[64,512,128]{2,1,0:T(8,128)} %get-tuple-element.330, s32[1024]{0:T(1024)S(1)} %pad_clamp_fusion.7), kind=kCustom, calls=%fused_computation.1.clone.1 | custom fusion | bytes 8388672 | tf_op jit(solution)/shard_map/cond/branch_0_fun/while/body/eval_jaxpr/jit(_take)/gather | solution.py:71
  570.1 21.5 %fusion.114 = f32[4,512,128]{2,1,0:T(8,128)} fusion(f32[4,512,128]{2,1,0:T(8,128)} %get-tuple-element.314, s32[]{:T(128)} %get-tuple-element.313, f32[16,512,128]{2,1,0:T(8,128)} %gather_fusion.2, pred[16]{0:T(512)(128)(4,1)S(1)} %compare_and_fusion.7, f32[512,16,512]{2,0,1:T(8,128)} %fusion.112, f32[16,512]{1,0:T(8,128)S(1)} %multiply_reduce_fusion.5, ...), kind=kOutput, calls=%fused_computation.25.clone.1 | convolution fusion | flops 6464471040 | bytes 21269008 | tf_op jit(solution)/shard_map/cond/branch_0_fun/while/body/eval_jaxpr/tjs,jsw->tw/dot_general | solution.py:14
  591.6 0.6 dynamic_slice.65
  594.1 1.3 constant_dynamic-slice_fusion.9
  595.4 4.1 gather_fusion.3
  599.5 16.2 %fusion.112 = f32[512,16,512]{2,0,1:T(8,128)} fusion(f32[16,64,512]{2,1,0:T(8,128)S(1)} %gather_fusion.3, pred[16]{0:T(512)(128)(4,1)S(1)} %compare_and_fusion.7, f32[64,1,512]{2,1,0:T(1,128)S(1)} %constant_dynamic-slice_fusion.9, pred[]{:T(512)S(6)} %and.57), kind=kOutput, calls=%fused_computation.22.clone.1 | convolution fusion | flops 3221782528 | bytes 19005456 | tf_op jit(solution)/shard_map/cond/branch_0_fun/while/body/eval_jaxpr/dt,jds->tjs/dot_general | solution.py:9
  615.7 0.4 multiply_reduce_fusion.5
  616.1 8.5 %gather_fusion.2 = f32[16,512,128]{2,1,0:T(8,128)} fusion(f32[64,512,128]{2,1,0:T(8,128)} %get-tuple-element.330, s32[1024]{0:T(1024)S(1)} %pad_clamp_fusion.7), kind=kCustom, calls=%fused_computation.1.clone.1 | custom fusion | bytes 8388672 | tf_op jit(solution)/shard_map/cond/branch_0_fun/while/body/eval_jaxpr/jit(_take)/gather | solution.py:71
  624.6 21.5 %fusion.114 = f32[4,512,128]{2,1,0:T(8,128)} fusion(f32[4,512,128]{2,1,0:T(8,128)} %get-tuple-element.314, s32[]{:T(128)} %get-tuple-element.313, f32[16,512,128]{2,1,0:T(8,128)} %gather_fusion.2, pred[16]{0:T(512)(128)(4,1)S(1)} %compare_and_fusion.7, f32[512,16,512]{2,0,1:T(8,128)} %fusion.112, f32[16,512]{1,0:T(8,128)S(1)} %multiply_reduce_fusion.5, ...), kind=kOutput, calls=%fused_computation.25.clone.1 | convolution fusion | flops 6464471040 | bytes 21269008 | tf_op jit(solution)/shard_map/cond/branch_0_fun/while/body/eval_jaxpr/tjs,jsw->tw/dot_general | solution.py:14
  646.2 0.6 dynamic_slice.65
  648.6 1.3 constant_dynamic-slice_fusion.9
  650.0 4.1 gather_fusion.3
  654.1 16.2 %fusion.112 = f32[512,16,512]{2,0,1:T(8,128)} fusion(f32[16,64,512]{2,1,0:T(8,128)S(1)} %gather_fusion.3, pred[16]{0:T(512)(128)(4,1)S(1)} %compare_and_fusion.7, f32[64,1,512]{2,1,0:T(1,128)S(1)} %constant_dynamic-slice_fusion.9, pred[]{:T(512)S(6)} %and.57), kind=kOutput, calls=%fused_computation.22.clone.1 | convolution fusion | flops 3221782528 | bytes 19005456 | tf_op jit(solution)/shard_map/cond/branch_0_fun/while/body/eval_jaxpr/dt,jds->tjs/dot_general | solution.py:9
  670.3 0.4 multiply_reduce_fusion.5
  670.7 8.5 %gather_fusion.2 = f32[16,512,128]{2,1,0:T(8,128)} fusion(f32[64,512,128]{2,1,0:T(8,128)} %get-tuple-element.330, s32[1024]{0:T(1024)S(1)} %pad_clamp_fusion.7), kind=kCustom, calls=%fused_computation.1.clone.1 | custom fusion | bytes 8388672 | tf_op jit(solution)/shard_map/cond/branch_0_fun/while/body/eval_jaxpr/jit(_take)/gather | solution.py:71
  679.2 21.5 %fusion.114 = f32[4,512,128]{2,1,0:T(8,128)} fusion(f32[4,512,128]{2,1,0:T(8,128)} %get-tuple-element.314, s32[]{:T(128)} %get-tuple-element.313, f32[16,512,128]{2,1,0:T(8,128)} %gather_fusion.2, pred[16]{0:T(512)(128)(4,1)S(1)} %compare_and_fusion.7, f32[512,16,512]{2,0,1:T(8,128)} %fusion.112, f32[16,512]{1,0:T(8,128)S(1)} %multiply_reduce_fusion.5, ...), kind=kOutput, calls=%fused_computation.25.clone.1 | convolution fusion | flops 6464471040 | bytes 21269008 | tf_op jit(solution)/shard_map/cond/branch_0_fun/while/body/eval_jaxpr/tjs,jsw->tw/dot_general | solution.py:14
  700.7 2.0 broadcast.190
  702.7 2.3 constant_dynamic-update-slice_fusion
  705.0 0.0 all-reduce.4.cloned.1.call-update
  705.0 104.8 %all-reduce.4.cloned.1.call-done = f32[6144,128]{1,0:T(8,128)} async-done(((f32[6144,128]{1,0:T(8,128)}), f32[6144,128]{1,0:T(8,128)}) %all-reduce.4.cloned.1.call-update) | async-done | bytes 3145744 | tf_op jit(solution)/shard_map/psum | solution.py:92
  809.8 3.8 copy.95
  (35 shorter events, 0.3 us)
Async XLA Ops:
  6.5 37.7 %copy-start = (f32[6144,128]{1,0:T(8,128)S(1)}, f32[6144,128]{1,0:T(8,128)}, u32[]{:S(2)}) copy-start(f32[6144,128]{1,0:T(8,128)} %param.16) | copy-start | bytes 9437188
  8.1 16.4 %all-to-all-start = ((s32[32,1,2]{2,1,0:T(1,128)}), s32[32,1,2]{2,1,0:T(1,128)S(1)}, u32[]{:S(2)}, u32[]{:S(2)}) async-start(s32[32,1,2]{2,1,0:T(1,128)} %copy.36), calls=%async_computation | async-start | bytes 32768 | tf_op jit(solution)/shard_map/all_to_all | solution.py:33
  39.1 105.0 %all-to-all-start.1 = ((f32[32,2,64,512]{3,2,1,0:T(8,128)}), f32[32,2,64,512]{3,2,1,0:T(8,128)}, u32[]{:S(2)}, u32[]{:S(2)}) async-start(f32[32,2,64,512]{3,2,1,0:T(8,128)} %broadcast_select_fusion.1), calls=%async_computation.1 | async-start | bytes 16777216 | tf_op jit(solution)/shard_map/all_to_all | solution.py:36
  144.0 337.7 %all-to-all-start.2 = ((f32[32,2,512,128]{3,2,1,0:T(8,128)}), f32[32,2,512,128]{3,2,1,0:T(8,128)}, u32[]{:S(2)}, u32[]{:S(2)}) async-start(f32[32,2,512,128]{3,2,1,0:T(8,128)} %broadcast_select_fusion), calls=%async_computation.2 | async-start | bytes 33554432 | tf_op jit(solution)/shard_map/all_to_all | solution.py:37
  155.3 3.3 copy-start.4
  155.3 326.4 %all-reduce.6.cloned.1.call-start = ((), (), s32[]{:S(2)}) async-start(), calls=%async_computation.4 | async-start | bytes 12582912 | tf_op jit(solution)/shard_map/psum | solution.py:59
  167.2 2.3 copy-start.2
  169.4 312.3 %copy-start.3 = (s32[12,8]{0,1:T(8,128)S(1)}, s32[12,8]{0,1:T(8,128)}, u32[]{:S(2)}) copy-start(s32[12,8]{0,1:T(8,128)} %param.20) | copy-start | bytes 1156
  169.5 640.3 %all-reduce.4.cloned.1.call-start = ((), (), s32[]{:S(2)}) async-start(), calls=%async_computation.3 | async-start | bytes 6291456 | tf_op jit(solution)/shard_map/psum | solution.py:92
  705.0 108.6 %copy-start.1 = (f32[6144,128]{1,0:T(8,128)S(1)}, f32[6144,128]{1,0:T(8,128)}, u32[]{:S(2)}) copy-start(f32[6144,128]{1,0:T(8,128)} %param.16) | copy-start | bytes 9437188
Sparse Core Ops, SparseCore 0:
  169.6 312.1 all-reduce.5
  705.1 104.6 all-reduce.3
where the time goes:
time: 823 us; the launch traced here: 820 us
  waiting for transfers between devices  500 us (61%)
  matrix products  154 us (19%)
  local copies, waits for them, and re-layouts  96.2 us (12%)
  starting transfers between devices  26 us (3%)
  other arithmetic  22.5 us (3%)
  between operations  13.5 us (2%)
    psum x1, waiting for transfers between devices, on_device(): lax.psum((table_coords, table_weights), ('grp', 'dev'))  310 us
    psum x1, waiting for transfers between devices, on_device(): total = lax.psum(contribution, 'grp')  105 us
    dot_general x4, matrix products, kernel_sum(): return jnp.einsum('tjs,jsw->tw', kernel, values, precision=high)  86.1 us
    all_to_all x1, waiting for transfers between devices, on_device(): lax.all_to_all(coords, 'dev', split_axis=0, concat_axis=0, tiled=True)  80.8 us
    dot_general x4, matrix products, kernel_sum(): inner = jnp.einsum('dt,jds->tjs', target, sources, precision=high)  64.7 us
    gather x4, local copies, waits for them, and re-layouts, near_leaf(): jnp.take(flat_values, leaf_slots, axis=0)  34 us
  transfers between devices with their start and end apart: 5, of which 4 were waited for; matrix products, arithmetic and copies ran while one was open for 5% of the time, Pallas kernels for 0%

commit v1 on v0

--- a/solution.py
+++ b/solution.py
@@ -56,7 +56,7 @@
     )
     table_weights = jnp.zeros((devices, skeleton, columns), jnp.float32)
     table_weights = lax.dynamic_update_index_in_dim(table_weights, partial_value, node_index, 0)
-    skel_coords, skel_weights = lax.psum((table_coords, table_weights), ("grp", "dev"))
+    skel_coords, skel_weights = lax.psum(lax.psum((table_coords, table_weights), "dev"), "grp")
 
     def near_work():
         slots = lax.dynamic_slice_in_dim(near_list, near_row * row_leaves, row_leaves, 0)

time: 823 us -> 922 us (1.12)
  waiting for transfers between devices: 500 us -> 600 us
    psum x1 -> x2, waiting for transfers between devices: 310 us -> 408 us  [the longest x1 281 us: on_device(): lax.psum((table_coords, table_weights), 'dev')]
  transfers between devices with their start and end apart: 5 -> 6, of which waited for: 4 -> 5; matrix products, arithmetic and copies ran while one was open for 5% -> 4% of each run, Pallas kernels for 0% -> 0%
where the time goes in v1:
time: 922 us; the launch traced here: 920 us
  waiting for transfers between devices  600 us (65%)
  matrix products  154 us (17%)
  local copies, waits for them, and re-layouts  96.3 us (10%)
  starting transfers between devices  26 us (3%)
  other arithmetic  21.9 us (2%)
  between operations  13.2 us (1%)
    psum x1, waiting for transfers between devices, on_device(): lax.psum((table_coords, table_weights), 'dev')  281 us
    psum x1, waiting for transfers between devices, on_device(): lax.psum(lax.psum((table_coords, table_weights), 'dev'), 'grp')  127 us
    psum x1, waiting for transfers between devices, on_device(): total = lax.psum(contribution, 'grp')  107 us
    dot_general x4, matrix products, kernel_sum(): return jnp.einsum('tjs,jsw->tw', kernel, values, precision=high)  86.1 us
    all_to_all x1, waiting for transfers between devices, on_device(): lax.all_to_all(coords, 'dev', split_axis=0, concat_axis=0, tiled=True)  80.8 us
    dot_general x4, matrix products, kernel_sum(): inner = jnp.einsum('dt,jds->tjs', target, sources, precision=high)  64.8 us
    gather x4, local copies, waits for them, and re-layouts, near_leaf(): jnp.take(flat_values, leaf_slots, axis=0)  34 us
  transfers between devices with their start and end apart: 6, of which 5 were waited for; matrix products, arithmetic and copies ran while one was open for 4% of the time, Pallas kernels for 0%

profile of v1, /device:TPU:1, one launch (start us, length us, event | category | flops | bytes accessed | tf_op | source)
XLA Modules:
  0.0 919.9 jit_solution(17287666366126362514)
XLA Ops:
  6.5 0.8 fusion.82
  7.4 0.7 copy.36
  8.1 9.4 %all-to-all-start = ((s32[32,1,2]{2,1,0:T(1,128)}), s32[32,1,2]{2,1,0:T(1,128)S(1)}, u32[]{:S(2)}, u32[]{:S(2)}) async-start(s32[32,1,2]{2,1,0:T(1,128)} %copy.36), calls=%async_computation | async-start | bytes 32768 | tf_op jit(solution)/shard_map/all_to_all | solution.py:33
  17.5 2.7 copy.64
  20.2 4.2 all-to-all-done
  24.4 0.1 copy.37
  24.5 0.1 copy.40
  24.6 0.1 reshape.285
  24.7 0.1 copy.38
  24.8 5.7 gather_fusion.4
  30.6 8.5 broadcast_select_fusion.1
  39.1 5.2 all-to-all-start.1
  44.3 7.4 gather_fusion.5
  51.6 11.6 %broadcast_select_fusion = f32[32,2,512,128]{3,2,1,0:T(8,128)} fusion(f32[32,2,512,128]{3,2,1,0:T(8,128)} %bitcast.101, pred[32,2]{1,0:T(8,128)(4,1)S(1)} %copy.38), kind=kLoop, calls=%fused_computation.86 | loop fusion | flops 4194304 | bytes 33554496 | tf_op jit(solution)/shard_map/jit(_take)/select_n | solution.py:35
  63.2 80.8 %all-to-all-done.1 = f32[32,2,64,512]{3,2,1,0:T(8,128)} async-done(((f32[32,2,64,512]{3,2,1,0:T(8,128)}), f32[32,2,64,512]{3,2,1,0:T(8,128)}, u32[]{:S(2)}, u32[]{:S(2)}) %all-to-all-start.1) | async-done | bytes 8388640 | tf_op jit(solution)/shard_map/all_to_all | solution.py:36
  144.0 11.3 %all-to-all-start.2 = ((f32[32,2,512,128]{3,2,1,0:T(8,128)}), f32[32,2,512,128]{3,2,1,0:T(8,128)}, u32[]{:S(2)}, u32[]{:S(2)}) async-start(f32[32,2,512,128]{3,2,1,0:T(8,128)} %broadcast_select_fusion), calls=%async_computation.2 | async-start | bytes 33554432 | tf_op jit(solution)/shard_map/all_to_all | solution.py:37
  155.3 0.0 all-reduce.8.cloned.1.call-start
  155.4 3.3 copy.43
  158.7 2.6 gather_fusion.6
  161.3 0.1 copy.44
  161.4 2.4 broadcast_in_dim.110
  163.8 3.5 fusion.75
  167.3 0.2 broadcast_in_dim.107
  167.6 1.3 copy-done.3
  168.9 0.0 all-reduce.10.cloned.1.call-start
  169.0 280.7 %all-reduce.8.cloned.1.call-done = (f32[32,64,256]{2,1,0:T(8,128)}, f32[32,256,128]{2,1,0:T(8,128)}) async-done(((f32[32,64,256]{2,1,0:T(8,128)}, f32[32,256,128]{2,1,0:T(8,128)}), (f32[32,64,256]{2,1,0:T(8,128)}, f32[32,256,128]{2,1,0:T(8,128)})) %all-reduce.8.cloned.1.call-update) | async-done | bytes 6291472 | tf_op jit(solution)/shard_map/psum | solution.py:59
  449.7 0.0 all-reduce.6.cloned.1.call-start
  449.8 1.9 reshape.193
  451.7 127.1 %all-reduce.10.cloned.1.call-done = (f32[32,64,256]{2,1,0:T(8,128)}, f32[32,256,128]{2,1,0:T(8,128)}) async-done(((f32[32,64,256]{2,1,0:T(8,128)}, f32[32,256,128]{2,1,0:T(8,128)}), (f32[32,64,256]{2,1,0:T(8,128)}, f32[32,256,128]{2,1,0:T(8,128)})) %all-reduce.10.cloned.1.call-update) | async-done | bytes 6291472 | tf_op jit(solution)/shard_map/psum | solution.py:59
  578.8 223.3 %conditional.1 = (f32[12,512,128]{2,1,0:T(8,128)}) conditional(s32[]{:T(128)} %convert_element_type.3, (s32[]{:T(128)}, s32[12,16]{1,0:T(8,128)}, f32[32,2,64,512]{3,2,1,0:T(8,128)}, f32[32,2,512,128]{3,2,1,0:T(8,128)}, f32[64,12,512]{2,1,0:T(8,128)}) %tuple.20, (f32[64,12,512]{2,1,0:T(8,128)}, s32[12,8]{0,1:T(8,128)S(1)}, ...), branch_computations={%region_4.10_spmd, %region_9.15_spmd} | conditional | flops 9687917568 | bytes 60630836 | solution.py:91
  578.8 0.7 constant_dynamic-slice_fusion.2
  579.5 218.4 %while.19 = (s32[]{:T(128)}, f32[4,512,128]{2,1,0:T(8,128)}, s32[4]{0:T(128)S(1)}, f32[64,12,512]{2,1,0:T(8,128)}, s32[4,16]{1,0:T(4,128)S(1)}, /*index=5*/f32[6...) while((s32[]{:T(128)}, f32[4,512,128]{2,1,0:T(8,128)}, ...), condition=%wide.region_8.9_spmd, body=%wide.region_5.8_spmd.sunk | while | flops 9687917568 | bytes 55387260 | solution.py:74
  579.5 0.6 dynamic_slice.65
  582.0 1.3 constant_dynamic-slice_fusion.9
  583.3 4.1 gather_fusion.3
  587.4 16.2 %fusion.112 = f32[512,16,512]{2,0,1:T(8,128)} fusion(f32[16,64,512]{2,1,0:T(8,128)S(1)} %gather_fusion.3, pred[16]{0:T(512)(128)(4,1)S(1)} %compare_and_fusion.7, f32[64,1,512]{2,1,0:T(1,128)S(1)} %constant_dynamic-slice_fusion.9, pred[]{:T(512)S(6)} %and.57), kind=kOutput, calls=%fused_computation.22.clone.1 | convolution fusion | flops 3221782528 | bytes 19005456 | tf_op jit(solution)/shard_map/cond/branch_0_fun/while/body/eval_jaxpr/dt,jds->tjs/dot_general | solution.py:9
  603.7 0.4 multiply_reduce_fusion.5
  604.0 8.5 gather_fusion.2
  612.5 21.5 %fusion.114 = f32[4,512,128]{2,1,0:T(8,128)} fusion(f32[4,512,128]{2,1,0:T(8,128)} %get-tuple-element.316, s32[]{:T(128)} %get-tuple-element.315, f32[16,512,128]{2,1,0:T(8,128)} %gather_fusion.2, pred[16]{0:T(512)(128)(4,1)S(1)} %compare_and_fusion.7, f32[512,16,512]{2,0,1:T(8,128)} %fusion.112, f32[16,512]{1,0:T(8,128)S(1)} %multiply_reduce_fusion.5, ...), kind=kOutput, calls=%fused_computation.25.clone.1 | convolution fusion | flops 6464471040 | bytes 21269008 | tf_op jit(solution)/shard_map/cond/branch_0_fun/while/body/eval_jaxpr/tjs,jsw->tw/dot_general | solution.py:14
  634.1 0.6 dynamic_slice.65
  636.5 1.3 constant_dynamic-slice_fusion.9
  637.9 4.1 gather_fusion.3
  642.0 16.2 %fusion.112 = f32[512,16,512]{2,0,1:T(8,128)} fusion(f32[16,64,512]{2,1,0:T(8,128)S(1)} %gather_fusion.3, pred[16]{0:T(512)(128)(4,1)S(1)} %compare_and_fusion.7, f32[64,1,512]{2,1,0:T(1,128)S(1)} %constant_dynamic-slice_fusion.9, pred[]{:T(512)S(6)} %and.57), kind=kOutput, calls=%fused_computation.22.clone.1 | convolution fusion | flops 3221782528 | bytes 19005456 | tf_op jit(solution)/shard_map/cond/branch_0_fun/while/body/eval_jaxpr/dt,jds->tjs/dot_general | solution.py:9
  658.3 0.4 multiply_reduce_fusion.5
  658.6 8.5 gather_fusion.2
  667.1 21.5 %fusion.114 = f32[4,512,128]{2,1,0:T(8,128)} fusion(f32[4,512,128]{2,1,0:T(8,128)} %get-tuple-element.316, s32[]{:T(128)} %get-tuple-element.315, f32[16,512,128]{2,1,0:T(8,128)} %gather_fusion.2, pred[16]{0:T(512)(128)(4,1)S(1)} %compare_and_fusion.7, f32[512,16,512]{2,0,1:T(8,128)} %fusion.112, f32[16,512]{1,0:T(8,128)S(1)} %multiply_reduce_fusion.5, ...), kind=kOutput, calls=%fused_computation.25.clone.1 | convolution fusion | flops 6464471040 | bytes 21269008 | tf_op jit(solution)/shard_map/cond/branch_0_fun/while/body/eval_jaxpr/tjs,jsw->tw/dot_general | solution.py:14
  688.7 0.6 dynamic_slice.65
  691.1 1.3 constant_dynamic-slice_fusion.9
  692.5 4.1 gather_fusion.3
  696.6 16.2 %fusion.112 = f32[512,16,512]{2,0,1:T(8,128)} fusion(f32[16,64,512]{2,1,0:T(8,128)S(1)} %gather_fusion.3, pred[16]{0:T(512)(128)(4,1)S(1)} %compare_and_fusion.7, f32[64,1,512]{2,1,0:T(1,128)S(1)} %constant_dynamic-slice_fusion.9, pred[]{:T(512)S(6)} %and.57), kind=kOutput, calls=%fused_computation.22.clone.1 | convolution fusion | flops 3221782528 | bytes 19005456 | tf_op jit(solution)/shard_map/cond/branch_0_fun/while/body/eval_jaxpr/dt,jds->tjs/dot_general | solution.py:9
  712.8 0.4 multiply_reduce_fusion.5
  713.2 8.5 gather_fusion.2
  721.7 21.5 %fusion.114 = f32[4,512,128]{2,1,0:T(8,128)} fusion(f32[4,512,128]{2,1,0:T(8,128)} %get-tuple-element.316, s32[]{:T(128)} %get-tuple-element.315, f32[16,512,128]{2,1,0:T(8,128)} %gather_fusion.2, pred[16]{0:T(512)(128)(4,1)S(1)} %compare_and_fusion.7, f32[512,16,512]{2,0,1:T(8,128)} %fusion.112, f32[16,512]{1,0:T(8,128)S(1)} %multiply_reduce_fusion.5, ...), kind=kOutput, calls=%fused_computation.25.clone.1 | convolution fusion | flops 6464471040 | bytes 21269008 | tf_op jit(solution)/shard_map/cond/branch_0_fun/while/body/eval_jaxpr/tjs,jsw->tw/dot_general | solution.py:14
  743.3 0.6 dynamic_slice.65
  745.7 1.3 constant_dynamic-slice_fusion.9
  747.1 4.1 gather_fusion.3
  751.2 16.2 %fusion.112 = f32[512,16,512]{2,0,1:T(8,128)} fusion(f32[16,64,512]{2,1,0:T(8,128)S(1)} %gather_fusion.3, pred[16]{0:T(512)(128)(4,1)S(1)} %compare_and_fusion.7, f32[64,1,512]{2,1,0:T(1,128)S(1)} %constant_dynamic-slice_fusion.9, pred[]{:T(512)S(6)} %and.57), kind=kOutput, calls=%fused_computation.22.clone.1 | convolution fusion | flops 3221782528 | bytes 19005456 | tf_op jit(solution)/shard_map/cond/branch_0_fun/while/body/eval_jaxpr/dt,jds->tjs/dot_general | solution.py:9
  767.5 0.4 multiply_reduce_fusion.5
  767.8 8.5 gather_fusion.2
  776.3 21.5 %fusion.114 = f32[4,512,128]{2,1,0:T(8,128)} fusion(f32[4,512,128]{2,1,0:T(8,128)} %get-tuple-element.316, s32[]{:T(128)} %get-tuple-element.315, f32[16,512,128]{2,1,0:T(8,128)} %gather_fusion.2, pred[16]{0:T(512)(128)(4,1)S(1)} %compare_and_fusion.7, f32[512,16,512]{2,0,1:T(8,128)} %fusion.112, f32[16,512]{1,0:T(8,128)S(1)} %multiply_reduce_fusion.5, ...), kind=kOutput, calls=%fused_computation.25.clone.1 | convolution fusion | flops 6464471040 | bytes 21269008 | tf_op jit(solution)/shard_map/cond/branch_0_fun/while/body/eval_jaxpr/tjs,jsw->tw/dot_general | solution.py:14
  797.9 2.0 broadcast.190
  799.8 2.3 constant_dynamic-update-slice_fusion
  802.1 107.5 %all-reduce.6.cloned.1.call-done = f32[6144,128]{1,0:T(8,128)} async-done(((f32[6144,128]{1,0:T(8,128)}), f32[6144,128]{1,0:T(8,128)}) %all-reduce.6.cloned.1.call-update) | async-done | bytes 3145744 | tf_op jit(solution)/shard_map/psum | solution.py:92
  909.6 3.8 copy.97
  (40 shorter events, 0.4 us)
Async XLA Ops:
  6.5 37.7 %copy-start = (f32[6144,128]{1,0:T(8,128)S(1)}, f32[6144,128]{1,0:T(8,128)}, u32[]{:S(2)}) copy-start(f32[6144,128]{1,0:T(8,128)} %param.16) | copy-start | bytes 9437188
  8.1 16.4 %all-to-all-start = ((s32[32,1,2]{2,1,0:T(1,128)}), s32[32,1,2]{2,1,0:T(1,128)S(1)}, u32[]{:S(2)}, u32[]{:S(2)}) async-start(s32[32,1,2]{2,1,0:T(1,128)} %copy.36), calls=%async_computation | async-start | bytes 32768 | tf_op jit(solution)/shard_map/all_to_all | solution.py:33
  39.1 105.0 %all-to-all-start.1 = ((f32[32,2,64,512]{3,2,1,0:T(8,128)}), f32[32,2,64,512]{3,2,1,0:T(8,128)}, u32[]{:S(2)}, u32[]{:S(2)}) async-start(f32[32,2,64,512]{3,2,1,0:T(8,128)} %broadcast_select_fusion.1), calls=%async_computation.1 | async-start | bytes 16777216 | tf_op jit(solution)/shard_map/all_to_all | solution.py:36
  144.0 434.7 %all-to-all-start.2 = ((f32[32,2,512,128]{3,2,1,0:T(8,128)}), f32[32,2,512,128]{3,2,1,0:T(8,128)}, u32[]{:S(2)}, u32[]{:S(2)}) async-start(f32[32,2,512,128]{3,2,1,0:T(8,128)} %broadcast_select_fusion), calls=%async_computation.2 | async-start | bytes 33554432 | tf_op jit(solution)/shard_map/all_to_all | solution.py:37
  155.3 3.3 copy-start.5
  155.3 294.4 %all-reduce.8.cloned.1.call-start = ((), (), s32[]{:S(2)}) async-start(), calls=%async_computation.4 | async-start | bytes 12582912 | tf_op jit(solution)/shard_map/psum | solution.py:59
  167.5 1.3 copy-start.3
  168.9 280.9 %copy-start.2 = (f32[64,6144]{1,0:T(8,128)S(1)}, f32[64,6144]{1,0:T(8,128)}, u32[]{:S(2)}) copy-start(f32[64,6144]{1,0:T(8,128)} %param.15) | copy-start | bytes 4718596
  168.9 409.9 %all-reduce.10.cloned.1.call-start = ((), (), s32[]{:S(2)}) async-start(), calls=%async_computation.5 | async-start | bytes 12582912 | tf_op jit(solution)/shard_map/psum | solution.py:59
  449.7 129.1 %copy-start.4 = (s32[12,8]{0,1:T(8,128)S(1)}, s32[12,8]{0,1:T(8,128)}, u32[]{:S(2)}) copy-start(s32[12,8]{0,1:T(8,128)} %param.20) | copy-start | bytes 1156
  449.7 459.9 %all-reduce.6.cloned.1.call-start = ((), (), s32[]{:S(2)}) async-start(), calls=%async_computation.3 | async-start | bytes 6291456 | tf_op jit(solution)/shard_map/psum | solution.py:92
  802.1 111.3 %copy-start.1 = (f32[6144,128]{1,0:T(8,128)S(1)}, f32[6144,128]{1,0:T(8,128)}, u32[]{:S(2)}) copy-start(f32[6144,128]{1,0:T(8,128)} %param.16) | copy-start | bytes 9437188
Sparse Core Ops, SparseCore 0:
  169.0 280.6 all-reduce.7
  452.1 126.6 all-reduce.9
  802.2 107.3 all-reduce.5
